TPU v7x, 32 devices: a whole 2x2x4 slice. The times are simulated.
32 devices in a mesh: groups: 2 (over x), fsdp: 16 (over z, y, core).
Axes of the slice: x: 2, y: 2, z: 4, core: 2. Of those that a mesh axis runs over, the one named last changes fastest.
Arguments:
- tokens: bfloat16 [4096, 8192], P(('groups', 'fsdp')), parts along dimension 0, may hold values from -6 to 6
- token_job_index: int32 [4096, 1], P(('groups', 'fsdp')), parts along dimension 0, may hold values from 0 to 15; in each aligned block of 128 rows (0 to 127, 128 to 255, ...) at most 10 rows name the same one
- frozen_value_weight: bfloat16 [8192, 1024], P('fsdp'), may hold values from -0.0625 to 0.0625
- output_gradient: bfloat16 [4096, 1024], P(('groups', 'fsdp')), parts along dimension 0, may hold values from -6 to 6
- down_factor: bfloat16 [32, 8192, 64], P(('groups', 'fsdp')), parts along dimension 0, may hold values from -0.0625 to 0.0625
- up_factor: bfloat16 [32, 64, 1024], P(('groups', 'fsdp')), parts along dimension 0, may hold values from -0.75 to 0.75
- job_adapter_rank: int32 [32], P(('groups', 'fsdp')), parts along dimension 0, may hold values from 16 to 64, as said below
Outputs:
- values: bfloat16 [4096, 1024], P(('groups', 'fsdp')), parts along dimension 0
- grad_in: bfloat16 [4096, 8192], P(('groups', 'fsdp')), parts along dimension 0
- down_gradient: float32 [32, 8192, 64], P(('groups', 'fsdp')), parts along dimension 0
- up_gradient: float32 [32, 64, 1024], P(('groups', 'fsdp')), parts along dimension 0
There are 2 independent parts, one for each index of `groups`. A program takes and returns all parts, laid end to end along the dimension named above; an argument that names none is the same for every part. Nothing has to cross between parts.
Inputs may be any that keep to these rules, and one draw needn't show every extreme that they name: `token_job_index`: among the 128 tokens of one device at most 10 belong to one job, and every job has tokens somewhere in the group. `job_adapter_rank`: ranks are multiples of 16.
All inputs are finite; a program needn't handle non-finite values.
Results may differ from a plain program's by a relative error of at most 0.0044.
Values may be sent and summed in bfloat16 or wider, within the bound.
A program may use at most 128 MiB of HBM per device.

v0:
```python
import jax
import jax.numpy as jnp
from jax import lax
from jax.sharding import PartitionSpec as P


def holder_forward(dispatched_input, down_matrix, up_matrix, adapter_rank_mask, adapter_scale):
    narrow_product = (
        jnp.dot(dispatched_input, down_matrix, preferred_element_type=jnp.float32)
        * adapter_rank_mask
    ).astype(jnp.bfloat16)
    adapter_output = (
        jnp.dot(narrow_product, up_matrix, preferred_element_type=jnp.float32) * adapter_scale
    ).astype(jnp.bfloat16)
    return (narrow_product, adapter_output)


def holder_backward(
    dispatched_input,
    dispatched_gradient,
    narrow_product,
    down_matrix,
    up_matrix,
    adapter_rank_mask,
    adapter_scale,
):
    narrow_gradient = lax.dot_general(
        dispatched_gradient, up_matrix, (((1,), (1,)), ((), ())), preferred_element_type=jnp.float32
    )
    narrow_gradient = (narrow_gradient * (adapter_scale * adapter_rank_mask)).astype(jnp.bfloat16)
    up_gradient = (
        lax.dot_general(
            narrow_product,
            dispatched_gradient,
            (((0,), (0,)), ((), ())),
            preferred_element_type=jnp.float32,
        )
        * adapter_scale
    )
    down_gradient = lax.dot_general(
        dispatched_input,
        narrow_gradient,
        (((0,), (0,)), ((), ())),
        preferred_element_type=jnp.float32,
    )
    adapter_backward = lax.dot_general(
        narrow_gradient, down_matrix, (((1,), (1,)), ((), ())), preferred_element_type=jnp.float32
    ).astype(jnp.bfloat16)
    return (down_gradient, up_gradient, adapter_backward)


def shards(
    tokens,
    token_job_index,
    frozen_value_weight,
    output_gradient,
    down_factor,
    up_factor,
    job_adapter_rank,
):
    group_size = lax.axis_size("fsdp")
    local_tokens = tokens.shape[0]
    capacity = 5 * local_tokens // (4 * group_size)
    slot_count = group_size * capacity
    job_ids = token_job_index[:, 0]
    onehot = (job_ids[:, None] == jnp.arange(group_size, dtype=jnp.int32)[None, :]).astype(
        jnp.float32
    )
    row_iota = jnp.arange(local_tokens, dtype=jnp.int32)
    strict_lower = (row_iota[:, None] > row_iota[None, :]).astype(jnp.float32)
    earlier = jnp.dot(
        strict_lower, onehot, precision=lax.Precision.HIGHEST, preferred_element_type=jnp.float32
    )
    position = jnp.sum(earlier * onehot, axis=1).astype(jnp.int32)
    slot = job_ids * capacity + position
    slot_match = slot[None, :] == jnp.arange(slot_count, dtype=jnp.int32)[:, None]
    filled = jnp.any(slot_match, axis=1)
    source = jnp.sum(jnp.where(slot_match, row_iota[None, :], 0), axis=1)
    send_x = jnp.where(filled[:, None], tokens[source], jnp.zeros((), tokens.dtype))
    send_g = jnp.where(
        filled[:, None], output_gradient[source], jnp.zeros((), output_gradient.dtype)
    )
    down_matrix = down_factor[0]
    up_matrix = up_factor[0]
    adapter_rank_value = job_adapter_rank[0]
    adapter_rank_mask = (jnp.arange(down_matrix.shape[1]) < adapter_rank_value).astype(jnp.float32)
    adapter_scale = 32.0 / adapter_rank_value.astype(jnp.float32)
    shard_rows = lax.all_gather(frozen_value_weight, "fsdp", axis=0, tiled=True)
    out_acc = jnp.dot(tokens, shard_rows, preferred_element_type=jnp.float32)
    partial_value = lax.dot_general(
        output_gradient, shard_rows, (((1,), (1,)), ((), ())), preferred_element_type=jnp.float32
    )
    dispatched_input = lax.all_to_all(send_x, "fsdp", split_axis=0, concat_axis=0, tiled=True)
    narrow_product, adapter_output = holder_forward(
        dispatched_input, down_matrix, up_matrix, adapter_rank_mask, adapter_scale
    )
    received_output = lax.all_to_all(
        adapter_output, "fsdp", split_axis=0, concat_axis=0, tiled=True
    )
    dispatched_gradient = lax.all_to_all(send_g, "fsdp", split_axis=0, concat_axis=0, tiled=True)
    down_gradient, up_gradient, adapter_backward = holder_backward(
        dispatched_input,
        dispatched_gradient,
        narrow_product,
        down_matrix,
        up_matrix,
        adapter_rank_mask,
        adapter_scale,
    )
    received_backward = lax.all_to_all(
        adapter_backward, "fsdp", split_axis=0, concat_axis=0, tiled=True
    )
    values = (out_acc + received_output[slot].astype(jnp.float32)).astype(jnp.bfloat16)
    grad_in = (partial_value + received_backward[slot].astype(jnp.float32)).astype(jnp.bfloat16)
    return (values, grad_in, down_gradient[None], up_gradient[None])


def solution(mesh):
    placed = (
        P(("groups", "fsdp"), None),
        P(("groups", "fsdp"), None),
        P("fsdp", None),
        P(("groups", "fsdp"), None),
        P(("groups", "fsdp"), None, None),
        P(("groups", "fsdp"), None, None),
        P(("groups", "fsdp")),
    )
    return jax.shard_map(
        shards,
        mesh=mesh,
        in_specs=placed,
        out_specs=(
            P(("groups", "fsdp"), None),
            P(("groups", "fsdp"), None),
            P(("groups", "fsdp"), None, None),
            P(("groups", "fsdp"), None, None),
        ),
        check_vma=False,
    )
```

profile of v0, /device:TPU:5, one launch (start us, length us, event | category | flops | bytes accessed | tf_op | source)
XLA Modules:
  0.0 372.6 jit_solution(10627348113274036255)
XLA Ops:
  7.2 0.0 copy-start
  7.2 0.0 copy-start.1
  7.2 0.0 all-gather.2.cloned.1.call-start
  7.2 0.7 all-gather.2.cloned.1.call-update
  7.9 0.9 fusion.6
  8.8 0.7 convert_add_fusion
  9.5 0.1 select_reduce_fusion
  9.6 0.0 copy-done.1
  9.6 0.9 gather_fusion.2
  10.6 0.1 gather.20
  10.7 0.1 fusion.11
  10.8 0.1 broadcast_in_dim.58
  10.9 0.9 broadcast_select_fusion.1
  11.8 6.7 %all-to-all-start.2 = ((bf16[16,10,1024]{2,1,0:T(8,128)(2,1)}), bf16[16,10,1024]{2,1,0:T(8,128)(2,1)}, u32[]{:S(2)}, u32[]{:S(2)}) async-start(bf16[16,10,1024]{2,1,0:T(8,128)(2,1)} %broadcast_select_fusion.1), calls=%async_computation.2 | async-start | bytes 1048576 | tf_op jit(solution)/shard_map/all_to_all | solution.py:100
  18.5 0.0 copy-done
  18.5 3.7 gather_fusion
  22.2 4.7 %gather.17 = bf16[16,10,8192]{2,1,0:T(8,128)(2,1)} reshape(bf16[160,8192]{1,0:T(8,128)(2,1)} %gather_fusion) | data formatting | bytes 5242880 | tf_op jit(solution)/shard_map/gather | solution.py:79
  26.9 4.5 %broadcast_select_fusion = bf16[16,10,8192]{2,1,0:T(8,128)(2,1)} fusion(bf16[16,10,8192]{2,1,0:T(8,128)(2,1)} %gather.17, pred[16,10]{1,0:T(8,128)(4,1)S(1)} %broadcast_in_dim.58), kind=kLoop, calls=%fused_computation.8 | loop fusion | flops 1310720 | bytes 5243040 | tf_op jit(solution)/shard_map/jit(_where)/select_n | solution.py:79
  31.4 0.0 copy-start.4
  31.4 0.0 copy-start.2
  31.4 10.3 %all-to-all-done.2 = bf16[16,10,1024]{2,1,0:T(8,128)(2,1)} async-done(((bf16[16,10,1024]{2,1,0:T(8,128)(2,1)}), bf16[16,10,1024]{2,1,0:T(8,128)(2,1)}, u32[]{:S(2)}, u32[]{:S(2)}) %all-to-all-start.2) | async-done | bytes 327712 | tf_op jit(solution)/shard_map/all_to_all | solution.py:100
  41.7 8.7 %all-to-all-start = ((bf16[16,10,8192]{2,1,0:T(8,128)(2,1)}), bf16[16,10,8192]{2,1,0:T(8,128)(2,1)}, u32[]{:S(2)}, u32[]{:S(2)}) async-start(bf16[16,10,8192]{2,1,0:T(8,128)(2,1)} %broadcast_select_fusion), calls=%async_computation | async-start | bytes 8388608 | tf_op jit(solution)/shard_map/all_to_all | solution.py:93
  51.2 1.9 all_to_all.34
  53.1 0.0 copy-done.4
  53.1 1.2 fusion.5
  54.3 0.0 copy-start.5
  54.3 0.6 copy-done.5
  54.9 0.0 copy-done.2
  54.9 2.4 convolution_convert_fusion
  57.3 4.8 %all_to_all.35 = bf16[16,10,8192]{2,1,0:T(8,128)(2,1)} reshape(bf16[160,8192]{1,0:T(8,128)(2,1)} %convolution_convert_fusion) | data formatting | bytes 5242880 | tf_op jit(solution)/shard_map/all_to_all | solution.py:110
  62.0 139.0 %all-to-all-done = bf16[16,10,8192]{2,1,0:T(8,128)(2,1)} async-done(((bf16[16,10,8192]{2,1,0:T(8,128)(2,1)}), bf16[16,10,8192]{2,1,0:T(8,128)(2,1)}, u32[]{:S(2)}, u32[]{:S(2)}) %all-to-all-start) | async-done | bytes 2621472 | tf_op jit(solution)/shard_map/all_to_all | solution.py:93
  201.1 26.9 %all-to-all-start.3 = ((bf16[16,10,8192]{2,1,0:T(8,128)(2,1)}), bf16[16,10,8192]{2,1,0:T(8,128)(2,1)}, u32[]{:S(2)}, u32[]{:S(2)}) async-start(bf16[16,10,8192]{2,1,0:T(8,128)(2,1)} %all_to_all.35), calls=%async_computation.3 | async-start | bytes 8388608 | tf_op jit(solution)/shard_map/all_to_all | solution.py:110
  228.0 4.8 %all_to_all.29 = bf16[160,8192]{1,0:T(8,128)(2,1)} reshape(bf16[16,10,8192]{2,1,0:T(8,128)(2,1)} %all-to-all-done) | data formatting | bytes 5242880 | tf_op jit(solution)/shard_map/all_to_all | solution.py:93
  232.8 0.0 copy-start.8
  232.8 2.7 fusion.4
  235.6 0.0 copy-start.7
  235.6 0.6 copy-done.7
  236.2 0.0 copy-start.3
  236.2 0.0 copy-start.6
  236.2 0.3 fusion.1
  236.4 0.9 all_to_all.30
  237.4 73.3 %all-to-all-done.3 = bf16[16,10,8192]{2,1,0:T(8,128)(2,1)} async-done(((bf16[16,10,8192]{2,1,0:T(8,128)(2,1)}), bf16[16,10,8192]{2,1,0:T(8,128)(2,1)}, u32[]{:S(2)}, u32[]{:S(2)}) %all-to-all-start.3) | async-done | bytes 2621472 | tf_op jit(solution)/shard_map/all_to_all | solution.py:110
  310.6 14.8 %all-to-all-start.1 = ((bf16[16,10,1024]{2,1,0:T(8,128)(2,1)}), bf16[16,10,1024]{2,1,0:T(8,128)(2,1)S(1)}, u32[]{:S(2)}, u32[]{:S(2)}) async-start(bf16[16,10,1024]{2,1,0:T(8,128)(2,1)} %all_to_all.30), calls=%async_computation.1 | async-start | bytes 1048576 | tf_op jit(solution)/shard_map/all_to_all | solution.py:97
  325.4 0.0 copy-done.8
  325.4 0.0 copy-done.3
  325.4 1.6 fusion.3
  327.1 0.0 copy-done.6
  327.1 3.6 convolution_bitcast_fusion
  330.7 4.7 %all_to_all.37 = bf16[160,8192]{1,0:T(8,128)(2,1)} reshape(bf16[16,10,8192]{2,1,0:T(8,128)(2,1)} %all-to-all-done.3) | data formatting | bytes 5242880 | tf_op jit(solution)/shard_map/all_to_all | solution.py:110
  335.4 7.2 %gather_fusion.3 = bf16[128,8192]{1,0:T(8,128)(2,1)} fusion(bf16[160,8192]{1,0:T(8,128)(2,1)} %all_to_all.37, s32[1024]{0:T(1024)S(1)} %pad_clamp_fusion), kind=kCustom, calls=%fused_computation.3 | custom fusion | bytes 4194816 | tf_op jit(solution)/shard_map/gather | solution.py:114
  342.6 0.0 all-to-all-done.1
  342.6 0.1 all_to_all.32
  342.7 0.9 gather_fusion.1
  343.6 0.0 all-gather.2.cloned.1.call-done
  343.6 13.3 %fusion = bf16[128,8192]{1,0:T(8,128)(2,1)} fusion(bf16[128,1024]{1,0:T(8,128)(2,1)S(1)} %copy-done.1, bf16[8192,1024]{1,0:T(8,128)(2,1)} %all-gather.2.cloned.1.call-done, bf16[128,8192]{1,0:T(8,128)(2,1)} %gather_fusion.3), kind=kOutput, calls=%fused_computation.6 | convolution fusion | flops 2150629376 | bytes 21233664 | tf_op jit(solution)/shard_map/dot_general | solution.py:90
  356.9 8.8 %fusion.2 = bf16[128,1024]{1,0:T(8,128)(2,1)} fusion(bf16[128,8192]{1,0:T(8,128)(2,1)S(1)} %copy-done, bf16[8192,1024]{1,0:T(8,128)(2,1)} %all-gather.2.cloned.1.call-done, bf16[128,1024]{1,0:T(8,128)(2,1)S(1)} %gather_fusion.1), kind=kOutput, calls=%fused_computation.12 | convolution fusion | flops 2147876864 | bytes 19398656 | tf_op jit(solution)/shard_map/dot_general | solution.py:89
  (6 shorter events, 0.0 us)
Async XLA Ops:
  7.2 11.3 %copy-start = (bf16[128,8192]{1,0:T(8,128)(2,1)S(1)}, bf16[128,8192]{1,0:T(8,128)(2,1)}, u32[]{:S(2)}) copy-start(bf16[128,8192]{1,0:T(8,128)(2,1)} %param.7) | copy-start | bytes 6291460
  7.2 2.4 copy-start.1
  7.2 336.4 %all-gather.2.cloned.1.call-start = ((), (), s32[]{:S(2)}) async-start(), calls=%async_computation.4 | async-start | bytes 17825792 | tf_op jit(solution)/shard_map/all_gather | solution.py:88
  11.8 29.9 %all-to-all-start.2 = ((bf16[16,10,1024]{2,1,0:T(8,128)(2,1)}), bf16[16,10,1024]{2,1,0:T(8,128)(2,1)}, u32[]{:S(2)}, u32[]{:S(2)}) async-start(bf16[16,10,1024]{2,1,0:T(8,128)(2,1)} %broadcast_select_fusion.1), calls=%async_computation.2 | async-start | bytes 1048576 | tf_op jit(solution)/shard_map/all_to_all | solution.py:100
  31.4 21.6 %copy-start.4 = (bf16[1,64,1024]{2,1,0:T(8,128)(2,1)S(1)}, bf16[1,64,1024]{2,1,0:T(8,128)(2,1)}, u32[]{:S(2)}) copy-start(bf16[1,64,1024]{2,1,0:T(8,128)(2,1)} %param.12) | copy-start | bytes 393220
  31.4 23.5 %copy-start.2 = (bf16[1,8192,64]{1,2,0:T(8,128)(2,1)S(1)}, bf16[1,8192,64]{1,2,0:T(8,128)(2,1)}, u32[]{:S(2)}) copy-start(bf16[1,8192,64]{1,2,0:T(8,128)(2,1)} %param.11) | copy-start | bytes 3145732
  41.7 159.3 %all-to-all-start = ((bf16[16,10,8192]{2,1,0:T(8,128)(2,1)}), bf16[16,10,8192]{2,1,0:T(8,128)(2,1)}, u32[]{:S(2)}, u32[]{:S(2)}) async-start(bf16[16,10,8192]{2,1,0:T(8,128)(2,1)} %broadcast_select_fusion), calls=%async_computation | async-start | bytes 8388608 | tf_op jit(solution)/shard_map/all_to_all | solution.py:93
  54.3 0.6 copy-start.5
  201.1 109.5 %all-to-all-start.3 = ((bf16[16,10,8192]{2,1,0:T(8,128)(2,1)}), bf16[16,10,8192]{2,1,0:T(8,128)(2,1)}, u32[]{:S(2)}, u32[]{:S(2)}) async-start(bf16[16,10,8192]{2,1,0:T(8,128)(2,1)} %all_to_all.35), calls=%async_computation.3 | async-start | bytes 8388608 | tf_op jit(solution)/shard_map/all_to_all | solution.py:110
  232.8 92.6 %copy-start.8 = (s32[128,1]{0,1:T(1,128)S(1)}, s32[128,1]{0,1:T(1,128)}, u32[]{:S(2)}) copy-start(s32[128,1]{0,1:T(1,128)} %param.8) | copy-start | bytes 1540
  235.6 0.6 copy-start.7
  236.2 89.3 %copy-start.3 = (bf16[160,1024]{1,0:T(8,128)(2,1)S(1)}, bf16[160,1024]{1,0:T(8,128)(2,1)}, u32[]{:S(2)}) copy-start(bf16[160,1024]{1,0:T(8,128)(2,1)} %all_to_all.34) | copy-start | bytes 983044
  236.2 90.9 %copy-start.6 = (bf16[160,64]{0,1:T(8,128)(2,1)S(1)}, bf16[160,64]{0,1:T(8,128)(2,1)}, u32[]{:S(2)}) copy-start(bf16[160,64]{0,1:T(8,128)(2,1)} %copy-done.5) | copy-start | bytes 61444
  310.6 31.9 %all-to-all-start.1 = ((bf16[16,10,1024]{2,1,0:T(8,128)(2,1)}), bf16[16,10,1024]{2,1,0:T(8,128)(2,1)S(1)}, u32[]{:S(2)}, u32[]{:S(2)}) async-start(bf16[16,10,1024]{2,1,0:T(8,128)(2,1)} %all_to_all.30), calls=%async_computation.1 | async-start | bytes 1048576 | tf_op jit(solution)/shard_map/all_to_all | solution.py:97
Sparse Core Ops, SparseCore 0:
  10.2 215.3 all-gather.1
where the time goes:
time: 374 us; the launch traced here: 373 us
  waiting for transfers between devices  223 us (60%)
  starting transfers between devices  57.1 us (15%)
  local copies, waits for them, and re-layouts  36.1 us (10%)
  matrix products  34.8 us (9%)
  between operations  14.9 us (4%)
  other arithmetic  6.36 us (2%)
    all_to_all x1, waiting for transfers between devices, shards(): lax.all_to_all(send_x, 'fsdp', split_axis=0, concat_axis=0, tiled=True)  139 us
    all_to_all x1, waiting for transfers between devices, shards(): lax.all_to_all(adapter_backward, 'fsdp', split_axis=0, concat_axis=0, til...  73.3 us
    all_to_all x1, starting transfers between devices, shards(): lax.all_to_all(adapter_backward, 'fsdp', split_axis=0, concat_axis=0, til...  26.9 us
    all_to_all x1, starting transfers between devices, shards(): lax.all_to_all(adapter_output, 'fsdp', split_axis=0, concat_axis=0, tiled...  14.8 us
    dot_general x1, matrix products, shards(): lax.dot_general(output_gradient, shard_rows, (((1,), (1,)), ((), ())), pr...  13.3 us
    all_to_all x1, waiting for transfers between devices, shards(): lax.all_to_all(send_g, 'fsdp', split_axis=0, concat_axis=0, tiled=True)  10.3 us
    all_to_all x2, local copies, waits for them, and re-layouts, shards(): lax.all_to_all(adapter_backward, 'fsdp', split_axis=0, concat_axis=0, til...  9.53 us
    dot_general x1, matrix products, shards(): out_acc = jnp.dot(tokens, shard_rows, preferred_element_type=jnp.float32)  8.81 us
  transfers between devices with their start and end apart: 5, of which 3 were waited for; matrix products, arithmetic and copies ran while one was open for 10% of the time, Pallas kernels for 0%

commit v1 on v0

v1 whole, which is shorter than its diff:
```python
import functools

import jax
import jax.numpy as jnp
import numpy as np
from jax import lax
from jax.experimental import pallas as pl
from jax.experimental.pallas import tpu as pltpu
from jax.sharding import PartitionSpec as P

CHUNKS = 8
PIECES = 2
BF16 = jnp.bfloat16
F32 = jnp.float32
MESH = pl.DeviceIdType.MESH


def dot(a, b, ca=1, cb=0):
    return lax.dot_general(a, b, (((ca,), (cb,)), ((), ())), preferred_element_type=F32)


def kernel(
    n,
    cap,
    rank_ref,
    jobc_ref,
    jobr_ref,
    keyc_ref,
    keyr_ref,
    foldc_ref,
    foldr_ref,
    chunk_ref,
    tok_ref,
    g_ref,
    w_ref,
    a_ref,
    up_ref,
    val_ref,
    gin_ref,
    da_ref,
    du_ref,
    wbuf,
    stack,
    send,
    recv,
    ret,
    back,
    acat,
    upst,
    lowx,
    lgx,
    gacc,
    vacc,
    wl_sem,
    w_send,
    w_recv,
    s_send,
    s_recv,
    r_send,
    r_recv,
):
    me = lax.axis_index("fsdp")
    rb = CHUNKS * cap
    gb = 4 * rb
    outer = n // 4
    slots = n * cap
    tl, width = tok_ref.shape
    wide = g_ref.shape[1]
    xw = width // CHUNKS
    gw = wide // CHUNKS
    rank_max = up_ref.shape[0]
    lanes = CHUNKS * rank_max
    rows = wbuf.shape[1]
    prow = rows // PIECES
    o, m, c = me // 4, lax.rem(me // 2, 2), lax.rem(me, 2)

    def idx(oo, mm, cc):
        return (oo * 2 + mm) * 2 + cc

    local = pltpu.make_async_copy(w_ref, wbuf.at[me], wl_sem)
    local.start()

    barrier = pltpu.get_barrier_semaphore()

    @pl.loop(1, n)
    def _(d):
        pl.semaphore_signal(
            barrier, inc=1, device_id={"fsdp": lax.rem(me + d, n)}, device_id_type=MESH
        )

    pl.semaphore_wait(barrier, n - 1)
    local.wait()

    def w_copy(shard, piece, kind, dest):
        part = wbuf.at[shard, pl.ds(piece * prow, prow)]
        return pltpu.make_async_remote_copy(
            src_ref=part,
            dst_ref=part,
            send_sem=w_send.at[kind, shard, piece],
            recv_sem=w_recv.at[shard, piece],
            device_id={"fsdp": dest},
            device_id_type=MESH,
        )

    def up_dest():
        return lax.rem(me + 4, n)

    def down_dest():
        return lax.rem(me + n - 4, n)

    mid = idx(o, 1 - m, c)
    core = idx(o, m, 1 - c)

    for p in range(PIECES):

        @pl.when(o + 1 < outer)
        def _():
            w_copy(me, p, 0, up_dest()).start()

        @pl.when(o > 0)
        def _():
            w_copy(me, p, 1, down_dest()).start()

    jc = jobc_ref[...]
    jr = jobr_ref[...]
    same = jc == jr
    ri = lax.broadcasted_iota(jnp.int32, (tl, tl), 0)
    ci = lax.broadcasted_iota(jnp.int32, (tl, tl), 1)
    one = jnp.where(same, 1.0, 0.0)
    pos_c = jnp.sum(jnp.where(ci < ri, one, 0.0), axis=1, keepdims=True).astype(jnp.int32)
    pos_r = jnp.sum(jnp.where(ri < ci, one, 0.0), axis=0, keepdims=True).astype(jnp.int32)
    slot_c = jc * cap + pos_c
    slot_r = jr * cap + pos_r

    for k in range(CHUNKS):
        stack[k * tl : (k + 1) * tl, :xw] = tok_ref[:, k * xw : (k + 1) * xw]
        stack[k * tl : (k + 1) * tl, xw:] = g_ref[:, k * gw : (k + 1) * gw]
    tok_key = jnp.concatenate([slot_r + k * slots for k in range(CHUNKS)], axis=1)

    def s_copy(j, k):
        return pltpu.make_async_remote_copy(
            src_ref=send.at[pl.ds(j * rb, rb)],
            dst_ref=recv.at[pl.ds(k * rb, rb)],
            send_sem=s_send.at[j],
            recv_sem=s_recv.at[k],
            device_id={"fsdp": j},
            device_id_type=MESH,
        )

    def r_copy(j, k):
        return pltpu.make_async_remote_copy(
            src_ref=ret.at[pl.ds(j * rb, rb)],
            dst_ref=back.at[pl.ds(k * rb, rb)],
            send_sem=r_send.at[j],
            recv_sem=r_recv.at[k],
            device_id={"fsdp": j},
            device_id_type=MESH,
        )

    def quad(i):
        return lax.rem(o + i, outer)

    @pl.loop(1, outer + 1)
    def _(i):
        q = quad(i)
        key = keyc_ref[...] + q * (4 * cap)
        sel = jnp.where(key == tok_key, 1.0, 0.0).astype(BF16)
        send[pl.ds(q * gb, gb), :] = dot(sel, stack[...]).astype(BF16)
        for e in range(4):
            j = q * 4 + e

            @pl.when(j != me)
            def _():
                s_copy(j, me).start()

            @pl.when(j == me)
            def _():
                recv[pl.ds(me * rb, rb), :] = send[pl.ds(me * rb, rb), :]

    for p in range(PIECES):
        w_copy(me, p, 2, mid).start()
        w_copy(me, p, 3, core).start()

    for k in range(CHUNKS):
        acat[:, k * rank_max : (k + 1) * rank_max] = a_ref[k * xw : (k + 1) * xw, :]
        upst[k * rank_max : (k + 1) * rank_max, :] = up_ref[:, k * gw : (k + 1) * gw]

    @pl.loop(1, outer)
    def _(s):
        for p in range(PIECES):

            @pl.when(o - s >= 0)
            def _():
                k = idx(o - s, m, c)
                w_copy(k, p, 0, me).wait_recv()

                @pl.when(o + 1 < outer)
                def _():
                    w_copy(k, p, 0, up_dest()).start()

                w_copy(k, p, 2, mid).start()
                w_copy(k, p, 3, core).start()

            @pl.when(o + s < outer)
            def _():
                k = idx(o + s, m, c)
                w_copy(k, p, 1, me).wait_recv()

                @pl.when(o > 0)
                def _():
                    w_copy(k, p, 1, down_dest()).start()

                w_copy(k, p, 2, mid).start()
                w_copy(k, p, 3, core).start()

    rank = rank_ref[0]
    scale = 32.0 / jnp.full((1, 128), rank, jnp.int32).astype(F32)
    lane = lax.broadcasted_iota(jnp.int32, (1, 128), 1)
    mask = jnp.where(lax.rem(lane, rank_max) < rank, 1.0, 0.0)
    lane_chunk = lax.broadcasted_iota(jnp.int32, (gb, lanes), 1) // rank_max
    diag = lane_chunk == chunk_ref[...]
    fold = jnp.where(foldc_ref[...] == foldr_ref[...], 1.0, 0.0).astype(BF16)
    half = lax.broadcasted_iota(jnp.int32, (gb, 128), 1) < rank_max

    def narrow(y):
        y = jnp.where(diag, y, 0.0)
        z = y[:, :128]
        for k in range(1, lanes // 128):
            z = z + y[:, k * 128 : (k + 1) * 128]
        z = z + pltpu.roll(z, rank_max, 1)
        hi = z.astype(BF16).astype(F32)
        return jnp.where(half, hi, z - hi).astype(BF16)

    def widen(z):
        return jnp.where(diag, jnp.concatenate([z] * (lanes // 128), axis=1), 0.0).astype(BF16)

    @pl.loop(0, outer)
    def _(i):
        q = lax.rem(o + outer - i, outer)
        for e in range(4):
            j = q * 4 + e

            @pl.when(j != me)
            def _():
                s_copy(j, j).wait_recv()

        at = pl.ds(q * gb, gb)
        low = narrow(dot(recv[at, :xw], acat[...]))
        lg = narrow(dot(recv[at, xw:], upst[...], 1, 1))
        both = dot(fold, jnp.concatenate([low, lg], axis=1))
        low = both[:, :128]
        lg = both[:, 128:]
        low = ((low + pltpu.roll(low, rank_max, 1)) * mask).astype(BF16).astype(F32)
        lg = ((lg + pltpu.roll(lg, rank_max, 1)) * (scale * mask)).astype(BF16).astype(F32)
        low = widen(low)
        lg = widen(lg)
        lowx[at, :] = low
        lgx[at, :] = lg
        ret[at, :xw] = dot(lg, acat[...], 1, 1).astype(BF16)
        ret[at, xw:] = (dot(low, upst[...]) * scale[:, :1]).astype(BF16)
        for e in range(4):
            j = q * 4 + e

            @pl.when(j != me)
            def _():
                r_copy(j, me).start()

            @pl.when(j == me)
            def _():
                back[pl.ds(me * rb, rb), :] = ret[pl.ds(me * rb, rb), :]

    du = dot(lowx[...], recv[:, xw:], 0, 0) * scale[:, :1]
    for k in range(CHUNKS):
        du_ref[:, k * gw : (k + 1) * gw] = du[k * rank_max : (k + 1) * rank_max, :]

    for k in range(xw // 256):
        da = dot(recv[:, k * 256 : (k + 1) * 256], lgx[...], 0, 0)
        for e in range(CHUNKS):
            da_ref[pl.ds(e * xw + k * 256, 256), :] = da[:, e * rank_max : (e + 1) * rank_max]

    @pl.loop(0, outer)
    def _(s):
        for p in range(PIECES):

            @pl.when(o - s >= 0)
            def _():
                k = idx(o - s, 1 - m, c)
                w_copy(k, p, 2, me).wait_recv()
                w_copy(k, p, 3, core).start()

            @pl.when((s > 0) & (o + s < outer))
            def _():
                k = idx(o + s, 1 - m, c)
                w_copy(k, p, 2, me).wait_recv()
                w_copy(k, p, 3, core).start()

    vacc[...] = jnp.zeros_like(vacc)

    def product(k):
        cols = pl.ds(pl.multiple_of(k * rows, rows), rows)
        vacc[...] += dot(tok_ref[:, cols], wbuf[k])
        gacc[:, cols] = dot(g_ref[...], wbuf[k], 1, 1)

    @pl.loop(0, n // 2)
    def _(k):
        product(2 * k + c)

    @pl.loop(0, n // 2)
    def _(k):
        s = 2 * k + 1 - c
        for p in range(PIECES):
            w_copy(s, p, 3, me).wait_recv()
        product(s)

    @pl.loop(0, n)
    def _(j):
        @pl.when(j != me)
        def _():
            r_copy(j, j).wait_recv()

    vsum = jnp.zeros((tl, wide), F32)
    parts = []
    for k in range(CHUNKS):
        sel = jnp.where(slot_c + k * slots == keyr_ref[...], 1.0, 0.0).astype(BF16)
        add = dot(sel, back[...])
        cols = slice(k * xw, (k + 1) * xw)
        gin_ref[:, cols] = (gacc[:, cols] + add[:, :xw]).astype(BF16)
        vcols = slice(k * gw, (k + 1) * gw)
        val_ref[:, vcols] = (vacc[:, vcols] + add[:, xw:]).astype(BF16)

    @pl.loop(0, n)
    def _(j):
        @pl.when(j != me)
        def _():
            s_copy(j, me).wait_send()
            r_copy(j, me).wait_send()

    @pl.loop(0, outer)
    def _(z):
        for p in range(PIECES):
            k = idx(z, m, c)

            @pl.when((z <= o) & (o + 1 < outer))
            def _():
                w_copy(k, p, 0, up_dest()).wait_send()

            @pl.when((z >= o) & (o > 0))
            def _():
                w_copy(k, p, 1, down_dest()).wait_send()

            w_copy(k, p, 2, mid).wait_send()
            w_copy(k, p, 3, core).wait_send()
            w_copy(idx(z, 1 - m, c), p, 3, core).wait_send()


def shards(tokens, job, weight, gradient, down, up, rank):
    n = lax.axis_size("fsdp")
    tl, width = tokens.shape
    wide = gradient.shape[1]
    rank_max = up.shape[1]
    cap = 5 * tl // (4 * n)
    rb = CHUNKS * cap
    gb = 4 * rb
    total = n * rb
    xw, gw = width // CHUNKS, wide // CHUNKS
    lanes = CHUNKS * rank_max

    i = np.arange(total)
    key = (i % rb // cap) * (n * cap) + (i // rb) * cap + i % cap
    fold = (i // rb) * cap + i % cap
    consts = [
        key[:gb, None],
        key[None, :],
        fold[:gb, None],
        fold[None, :gb],
        (i % rb // cap)[:gb, None],
    ]
    consts = [jnp.asarray(v, jnp.int32) for v in consts]

    vmem = pl.BlockSpec(memory_space=pltpu.VMEM)
    args = (rank, job, job.reshape(1, tl), *consts, tokens, gradient, weight, down[0], up[0])
    specs = [pl.BlockSpec(memory_space=pltpu.SMEM)] + [vmem] * 9
    specs += [pl.BlockSpec(memory_space=pl.ANY)] + [vmem] * 2
    dma = pltpu.SemaphoreType.DMA
    values, grad_in, d_down, d_up = pl.pallas_call(
        functools.partial(kernel, n, cap),
        out_shape=(
            jax.ShapeDtypeStruct((tl, wide), BF16),
            jax.ShapeDtypeStruct((tl, width), BF16),
            jax.ShapeDtypeStruct((width, rank_max), F32),
            jax.ShapeDtypeStruct((rank_max, wide), F32),
        ),
        in_specs=specs,
        out_specs=(vmem,) * 4,
        scratch_shapes=[
            pltpu.VMEM((n, *weight.shape), BF16),
            pltpu.VMEM((CHUNKS * tl, xw + gw), BF16),
            pltpu.VMEM((total, xw + gw), BF16),
            pltpu.VMEM((total, xw + gw), BF16),
            pltpu.VMEM((total, xw + gw), BF16),
            pltpu.VMEM((total, xw + gw), BF16),
            pltpu.VMEM((xw, lanes), BF16),
            pltpu.VMEM((lanes, gw), BF16),
            pltpu.VMEM((total, lanes), BF16),
            pltpu.VMEM((total, lanes), BF16),
            pltpu.VMEM((tl, width), F32),
            pltpu.VMEM((tl, wide), F32),
            dma,
            dma((4, n, PIECES)),
            dma((n, PIECES)),
            dma((n,)),
            dma((n,)),
            dma((n,)),
            dma((n,)),
        ],
        compiler_params=pltpu.CompilerParams(
            collective_id=0, has_side_effects=True, vmem_limit_bytes=62 * 1024 * 1024
        ),
        cost_estimate=pl.CostEstimate(
            flops=16 * 10**9, bytes_accessed=16 * 2**20, transcendentals=0
        ),
    )(*args)
    return values, grad_in, d_down[None], d_up[None]


def solution(mesh):
    rows = P(("groups", "fsdp"), None)
    jobs = P(("groups", "fsdp"), None, None)
    return jax.shard_map(
        shards,
        mesh=mesh,
        in_specs=(rows, rows, P("fsdp", None), rows, jobs, jobs, P(("groups", "fsdp"))),
        out_specs=(rows, rows, jobs, jobs),
        check_vma=False,
    )
```

time: 374 us -> 230 us (0.61)
  waiting for transfers between devices: 223 us -> 0 us
  Pallas kernels: 0 us -> 218 us
  starting transfers between devices: 57.1 us -> 0 us
  matrix products: 34.8 us -> 0 us
  local copies, waits for them, and re-layouts: 36.1 us -> 10.8 us
  between operations: 14.9 us -> 1.31 us
  other arithmetic: 6.36 us -> 0 us
    all_to_all x4 -> x0, waiting for transfers between devices: 223 us -> none  [the longest x1 139 us: shards(): lax.all_to_all(send_x, 'fsdp', split_axis=0, concat_axis=0, tiled=True)]
    pallas_call x0 -> x1, Pallas kernels: none -> 218 us  [shards(): pl.pallas_call(functools.partial(kernel, n, cap), out_shape=(jax.ShapeDty...]
    all_to_all x4 -> x0, starting transfers between devices: 57.1 us -> none  [the longest x1 26.9 us: shards(): lax.all_to_all(adapter_backward, 'fsdp', split_axis=0, concat_axis=0, til...]
    dot_general x9 -> x0, matrix products: 34.8 us -> none  [the longest x1 13.3 us: shards(): lax.dot_general(output_gradient, shard_rows, (((1,), (1,)), ((), ())), pr...]
    gather x6 -> x0, local copies, waits for them, and re-layouts: 17.5 us -> none  [the longest x2 8.43 us: shards(): tokens[source]]
    all_to_all x6 -> x0, local copies, waits for them, and re-layouts: 17.2 us -> none  [the longest x2 9.53 us: shards(): lax.all_to_all(adapter_backward, 'fsdp', split_axis=0, concat_axis=0, til...]
    unnamed x18 -> x12, local copies, waits for them, and re-layouts: 1.25 us -> 10.8 us
    select_n x4 -> x0, other arithmetic: 5.43 us -> none  [the longest x1 4.5 us: shards(): jnp.where(filled[:, None], tokens[source], jnp.zeros((), tokens.dtype))]
  transfers between devices with their start and end apart: 5 -> 0, of which waited for: 3 -> 0; matrix products, arithmetic and copies ran while one was open for 10% -> 0% of each run, Pallas kernels for 0% -> 0%
where the time goes in v1:
time: 230 us
  Pallas kernels  218 us (95%)
  local copies, waits for them, and re-layouts  10.8 us (5%)
    pallas_call x1, Pallas kernels, shards(): pl.pallas_call(functools.partial(kernel, n, cap), out_shape=(jax.ShapeDty...  218 us
    unnamed x12, local copies, waits for them, and re-layouts  10.8 us

profile of v1, /device:TPU:5, one launch (start us, length us, event | category | flops | bytes accessed | tf_op | source)
XLA Modules:
  0.0 229.8 jit_solution(18239595688795416196)
XLA Ops:
  1.3 1.4 copy.17.jobc_ref
  2.7 2.7 %copy.16 = bf16[1,8192,64]{2,1,0:T(8,128)(2,1)} copy(bf16[1,8192,64]{1,2,0:T(8,128)(2,1)} %param.16) | data formatting | bytes 2097152 | tf_op args[4]
  5.4 217.7 %shard_map.147 = (bf16[128,1024]{1,0:T(8,128)(2,1)}, bf16[128,8192]{1,0:T(8,128)(2,1)}, f32[8192,64]{1,0:T(8,128)}, f32[64,1024]{1,0:T(8,128)}) custom-call(s32[1]{0:T(128)S(6)} %copy.22.rank_ref, s32[128,1]{1,0:T(8,128)} %copy.17.jobc_ref, s32[1,128]{1,0:T(1,128)} %bitcast.8, s32[320,1]{1,0:T(8,128)} %constant.10.clone.keyc_ref, ...), custom_call_target="tpu_custom_call" | custom-call | flops 16000000000 | bytes 16777216 | tf_op jit(solution)/shard_map/pallas_call | solution.py:385
  223.1 0.0 copy-start.2
  223.1 0.0 copy-start
  223.1 3.9 %copy.18 = f32[1,8192,64]{1,2,0:T(8,128)} copy(f32[1,8192,64]{2,1,0:T(8,128)} %bitcast.5) | data formatting | bytes 4194304
  227.0 0.0 copy-done.2
  227.0 0.7 copy.23
  227.7 0.0 copy-done
  227.7 0.0 copy-start.1
  227.7 1.3 copy.24
  229.1 0.0 copy-done.1
  229.1 0.7 copy.25
Async XLA Ops:
  223.1 4.0 %copy-start.2 = (bf16[128,1024]{1,0:T(8,128)(2,1)S(1)}, bf16[128,1024]{1,0:T(8,128)(2,1)}, u32[]{:S(2)}) copy-start(bf16[128,1024]{1,0:T(8,128)(2,1)} %get-tuple-element.20) | copy-start | bytes 786436
  223.1 4.7 %copy-start = (bf16[128,8192]{1,0:T(8,128)(2,1)S(1)}, bf16[128,8192]{1,0:T(8,128)(2,1)}, u32[]{:S(2)}) copy-start(bf16[128,8192]{1,0:T(8,128)(2,1)} %get-tuple-element.21) | copy-start | bytes 6291460
  227.7 1.3 copy-start.1

commit v2 on v1

--- a/solution.py
+++ b/solution.py
@@ -88,17 +88,27 @@
             barrier, inc=1, device_id={"fsdp": lax.rem(me + d, n)}, device_id_type=MESH
         )
 
-    pl.semaphore_wait(barrier, n - 1)
+    pair = lax.axis_size("groups") % 2 == 0
+    group = lax.axis_index("groups")
+    other = group + 1 - 2 * lax.rem(group, 2) if pair else group
+    mine = [lax.rem(group, 2)] if pair else list(range(PIECES))
+    theirs = [1 - lax.rem(group, 2)] if pair else []
+
+    if pair:
+        pl.semaphore_signal(
+            barrier, inc=1, device_id={"groups": other, "fsdp": me}, device_id_type=MESH
+        )
+    pl.semaphore_wait(barrier, n if pair else n - 1)
     local.wait()
 
     def w_copy(shard, piece, kind, dest):
-        part = wbuf.at[shard, pl.ds(piece * prow, prow)]
+        part = wbuf.at[shard, pl.ds(pl.multiple_of(piece * prow, prow), prow)]
         return pltpu.make_async_remote_copy(
             src_ref=part,
             dst_ref=part,
             send_sem=w_send.at[kind, shard, piece],
             recv_sem=w_recv.at[shard, piece],
-            device_id={"fsdp": dest},
+            device_id={"groups": other if kind == 4 else group, "fsdp": dest},
             device_id_type=MESH,
         )
 
@@ -111,15 +121,20 @@
     mid = idx(o, 1 - m, c)
     core = idx(o, m, 1 - c)
 
+    for p in mine:
+
+        @pl.when(o + 1 < outer)
+        def _():
+            w_copy(me, p, 0, up_dest()).start()
+
+        @pl.when(o > 0)
+        def _():
+            w_copy(me, p, 1, down_dest()).start()
+
+    for p in mine:
+        w_copy(me, p, 2, mid).start()
     for p in range(PIECES):
-
-        @pl.when(o + 1 < outer)
-        def _():
-            w_copy(me, p, 0, up_dest()).start()
-
-        @pl.when(o > 0)
-        def _():
-            w_copy(me, p, 1, down_dest()).start()
+        w_copy(me, p, 3, core).start()
 
     jc = jobc_ref[...]
     jr = jobr_ref[...]
@@ -166,6 +181,13 @@
         key = keyc_ref[...] + q * (4 * cap)
         sel = jnp.where(key == tok_key, 1.0, 0.0).astype(BF16)
         send[pl.ds(q * gb, gb), :] = dot(sel, stack[...]).astype(BF16)
+
+    for k in range(CHUNKS):
+        acat[k * rank_max : (k + 1) * rank_max, :] = a_ref[:, k * xw : (k + 1) * xw]
+        upst[k * rank_max : (k + 1) * rank_max, :] = up_ref[:, k * gw : (k + 1) * gw]
+
+    def dispatch(i):
+        q = quad(i)
         for e in range(4):
             j = q * 4 + e
 
@@ -177,17 +199,19 @@
             def _():
                 recv[pl.ds(me * rb, rb), :] = send[pl.ds(me * rb, rb), :]
 
-    for p in range(PIECES):
-        w_copy(me, p, 2, mid).start()
-        w_copy(me, p, 3, core).start()
-
-    for k in range(CHUNKS):
-        acat[:, k * rank_max : (k + 1) * rank_max] = a_ref[k * xw : (k + 1) * xw, :]
-        upst[k * rank_max : (k + 1) * rank_max, :] = up_ref[:, k * gw : (k + 1) * gw]
-
-    @pl.loop(1, outer)
+    def spread(k, p):
+        if pair:
+            w_copy(k, p, 4, me).start()
+        w_copy(k, p, 3, core).start()
+
+    def from_mid(k):
+        for p in mine:
+            w_copy(k, p, 2, me).wait_recv()
+            spread(k, p)
+
+    @pl.loop(1, outer + 1)
     def _(s):
-        for p in range(PIECES):
+        for p in mine:
 
             @pl.when(o - s >= 0)
             def _():
@@ -199,7 +223,7 @@
                     w_copy(k, p, 0, up_dest()).start()
 
                 w_copy(k, p, 2, mid).start()
-                w_copy(k, p, 3, core).start()
+                spread(k, p)
 
             @pl.when(o + s < outer)
             def _():
@@ -211,7 +235,23 @@
                     w_copy(k, p, 1, down_dest()).start()
 
                 w_copy(k, p, 2, mid).start()
-                w_copy(k, p, 3, core).start()
+                spread(k, p)
+
+        t = s - 1
+
+        @pl.when(o - t >= 0)
+        def _():
+            from_mid(idx(o - t, 1 - m, c))
+
+        @pl.when((t > 0) & (o + t < outer))
+        def _():
+            from_mid(idx(o + t, 1 - m, c))
+
+        @pl.when(s == 1)
+        def _():
+            @pl.loop(1, outer + 1)
+            def _(i):
+                dispatch(i)
 
     rank = rank_ref[0]
     scale = 32.0 / jnp.full((1, 128), rank, jnp.int32).astype(F32)
@@ -234,7 +274,7 @@
     def widen(z):
         return jnp.where(diag, jnp.concatenate([z] * (lanes // 128), axis=1), 0.0).astype(BF16)
 
-    @pl.loop(0, outer)
+    @pl.loop(1, outer + 1)
     def _(i):
         q = lax.rem(o + outer - i, outer)
         for e in range(4):
@@ -245,7 +285,7 @@
                 s_copy(j, j).wait_recv()
 
         at = pl.ds(q * gb, gb)
-        low = narrow(dot(recv[at, :xw], acat[...]))
+        low = narrow(dot(recv[at, :xw], acat[...], 1, 1))
         lg = narrow(dot(recv[at, xw:], upst[...], 1, 1))
         both = dot(fold, jnp.concatenate([low, lg], axis=1))
         low = both[:, :128]
@@ -256,7 +296,7 @@
         lg = widen(lg)
         lowx[at, :] = low
         lgx[at, :] = lg
-        ret[at, :xw] = dot(lg, acat[...], 1, 1).astype(BF16)
+        ret[at, :xw] = dot(lg, acat[...]).astype(BF16)
         ret[at, xw:] = (dot(low, upst[...]) * scale[:, :1]).astype(BF16)
         for e in range(4):
             j = q * 4 + e
@@ -274,32 +314,37 @@
         du_ref[:, k * gw : (k + 1) * gw] = du[k * rank_max : (k + 1) * rank_max, :]
 
     for k in range(xw // 256):
-        da = dot(recv[:, k * 256 : (k + 1) * 256], lgx[...], 0, 0)
+        da = dot(lgx[...], recv[:, k * 256 : (k + 1) * 256], 0, 0)
         for e in range(CHUNKS):
-            da_ref[pl.ds(e * xw + k * 256, 256), :] = da[:, e * rank_max : (e + 1) * rank_max]
-
-    @pl.loop(0, outer)
+            at = e * xw + k * 256
+            da_ref[:, at : at + 256] = da[e * rank_max : (e + 1) * rank_max, :]
+
+    def take(k):
+        for p in theirs:
+            w_copy(k, p, 4, me).wait_recv()
+            w_copy(k, p, 3, core).start()
+
+    @pl.loop(1, outer + 1)
     def _(s):
-        for p in range(PIECES):
-
-            @pl.when(o - s >= 0)
-            def _():
-                k = idx(o - s, 1 - m, c)
-                w_copy(k, p, 2, me).wait_recv()
-                w_copy(k, p, 3, core).start()
-
-            @pl.when((s > 0) & (o + s < outer))
-            def _():
-                k = idx(o + s, 1 - m, c)
-                w_copy(k, p, 2, me).wait_recv()
-                w_copy(k, p, 3, core).start()
+        for mm, t in ((m, s), (1 - m, s - 1)):
+
+            @pl.when(o - t >= 0)
+            def _():
+                take(idx(o - t, mm, c))
+
+            @pl.when((t > 0) & (o + t < outer))
+            def _():
+                take(idx(o + t, mm, c))
 
     vacc[...] = jnp.zeros_like(vacc)
+    gacc[:, xw:] = jnp.zeros((CHUNKS * tl, gw), F32)
 
     def product(k):
         cols = pl.ds(pl.multiple_of(k * rows, rows), rows)
         vacc[...] += dot(tok_ref[:, cols], wbuf[k])
-        gacc[:, cols] = dot(g_ref[...], wbuf[k], 1, 1)
+        at = pl.ds(pl.multiple_of(k * rows // xw * tl, tl), tl)
+        part = pl.ds(pl.multiple_of(lax.rem(k * rows, xw), rows), rows)
+        gacc[at, part] = dot(g_ref[...], wbuf[k], 1, 1)
 
     @pl.loop(0, n // 2)
     def _(k):
@@ -312,45 +357,59 @@
             w_copy(s, p, 3, me).wait_recv()
         product(s)
 
+    slot_key = jnp.concatenate([slot_c + k * slots for k in range(CHUNKS)], axis=0)
+
+    @pl.loop(1, outer + 1)
+    def _(i):
+        q = quad(i)
+        for e in range(4):
+            j = q * 4 + e
+
+            @pl.when(j != me)
+            def _():
+                r_copy(j, j).wait_recv()
+
+        sel = jnp.where(slot_key == keyr_ref[...] + q * (4 * cap), 1.0, 0.0).astype(BF16)
+        gacc[...] += dot(sel, back[pl.ds(q * gb, gb), :])
+
+    for k in range(CHUNKS):
+        at = slice(k * tl, (k + 1) * tl)
+        gin_ref[:, k * xw : (k + 1) * xw] = gacc[at, :xw].astype(BF16)
+        vcols = slice(k * gw, (k + 1) * gw)
+        val_ref[:, vcols] = (vacc[:, vcols] + gacc[at, xw:]).astype(BF16)
+
     @pl.loop(0, n)
     def _(j):
         @pl.when(j != me)
         def _():
-            r_copy(j, j).wait_recv()
-
-    vsum = jnp.zeros((tl, wide), F32)
-    parts = []
-    for k in range(CHUNKS):
-        sel = jnp.where(slot_c + k * slots == keyr_ref[...], 1.0, 0.0).astype(BF16)
-        add = dot(sel, back[...])
-        cols = slice(k * xw, (k + 1) * xw)
-        gin_ref[:, cols] = (gacc[:, cols] + add[:, :xw]).astype(BF16)
-        vcols = slice(k * gw, (k + 1) * gw)
-        val_ref[:, vcols] = (vacc[:, vcols] + add[:, xw:]).astype(BF16)
-
-    @pl.loop(0, n)
-    def _(j):
-        @pl.when(j != me)
-        def _():
             s_copy(j, me).wait_send()
             r_copy(j, me).wait_send()
 
     @pl.loop(0, outer)
     def _(z):
+        k = idx(z, m, c)
+        far = idx(z, 1 - m, c)
+        for p in mine:
+
+            @pl.when((z <= o) & (o + 1 < outer))
+            def _():
+                w_copy(k, p, 0, up_dest()).wait_send()
+
+            @pl.when((z >= o) & (o > 0))
+            def _():
+                w_copy(k, p, 1, down_dest()).wait_send()
+
+            w_copy(k, p, 2, mid).wait_send()
+            if pair:
+
+                @pl.when(z != o)
+                def _():
+                    w_copy(k, p, 4, me).wait_send()
+
+                w_copy(far, p, 4, me).wait_send()
         for p in range(PIECES):
-            k = idx(z, m, c)
-
-            @pl.when((z <= o) & (o + 1 < outer))
-            def _():
-                w_copy(k, p, 0, up_dest()).wait_send()
-
-            @pl.when((z >= o) & (o > 0))
-            def _():
-                w_copy(k, p, 1, down_dest()).wait_send()
-
-            w_copy(k, p, 2, mid).wait_send()
             w_copy(k, p, 3, core).wait_send()
-            w_copy(idx(z, 1 - m, c), p, 3, core).wait_send()
+            w_copy(far, p, 3, core).wait_send()
 
 
 def shards(tokens, job, weight, gradient, down, up, rank):
@@ -370,7 +429,7 @@
     fold = (i // rb) * cap + i % cap
     consts = [
         key[:gb, None],
-        key[None, :],
+        key[None, :gb],
         fold[:gb, None],
         fold[None, :gb],
         (i % rb // cap)[:gb, None],
@@ -378,7 +437,7 @@
     consts = [jnp.asarray(v, jnp.int32) for v in consts]
 
     vmem = pl.BlockSpec(memory_space=pltpu.VMEM)
-    args = (rank, job, job.reshape(1, tl), *consts, tokens, gradient, weight, down[0], up[0])
+    args = (rank, job, job.reshape(1, tl), *consts, tokens, gradient, weight, down[0].T, up[0])
     specs = [pl.BlockSpec(memory_space=pltpu.SMEM)] + [vmem] * 9
     specs += [pl.BlockSpec(memory_space=pl.ANY)] + [vmem] * 2
     dma = pltpu.SemaphoreType.DMA
@@ -387,7 +446,7 @@
         out_shape=(
             jax.ShapeDtypeStruct((tl, wide), BF16),
             jax.ShapeDtypeStruct((tl, width), BF16),
-            jax.ShapeDtypeStruct((width, rank_max), F32),
+            jax.ShapeDtypeStruct((rank_max, width), F32),
             jax.ShapeDtypeStruct((rank_max, wide), F32),
         ),
         in_specs=specs,
@@ -399,14 +458,14 @@
             pltpu.VMEM((total, xw + gw), BF16),
             pltpu.VMEM((total, xw + gw), BF16),
             pltpu.VMEM((total, xw + gw), BF16),
-            pltpu.VMEM((xw, lanes), BF16),
+            pltpu.VMEM((lanes, xw), BF16),
             pltpu.VMEM((lanes, gw), BF16),
             pltpu.VMEM((total, lanes), BF16),
             pltpu.VMEM((total, lanes), BF16),
-            pltpu.VMEM((tl, width), F32),
+            pltpu.VMEM((CHUNKS * tl, xw + gw), F32),
             pltpu.VMEM((tl, wide), F32),
             dma,
-            dma((4, n, PIECES)),
+            dma((5, n, PIECES)),
             dma((n, PIECES)),
             dma((n,)),
             dma((n,)),
@@ -420,7 +479,7 @@
             flops=16 * 10**9, bytes_accessed=16 * 2**20, transcendentals=0
         ),
     )(*args)
-    return values, grad_in, d_down[None], d_up[None]
+    return values, grad_in, d_down.T[None], d_up[None]
 
 
 def solution(mesh):

time: 230 us -> 180 us (0.78)
  Pallas kernels: 218 us -> 169 us
  local copies, waits for them, and re-layouts: 10.8 us -> 8.33 us
    pallas_call x1, Pallas kernels: 218 us -> 169 us  [shards(): pl.pallas_call(functools.partial(kernel, n, cap), out_shape=(jax.ShapeDty...]
    unnamed x12 -> x9, local copies, waits for them, and re-layouts: 10.8 us -> 8.33 us
where the time goes in v2:
time: 180 us; the launch traced here: 178 us
  Pallas kernels  169 us (94%)
  local copies, waits for them, and re-layouts  8.33 us (5%)
    pallas_call x1, Pallas kernels, shards(): pl.pallas_call(functools.partial(kernel, n, cap), out_shape=(jax.ShapeDty...  169 us
    unnamed x9, local copies, waits for them, and re-layouts  8.33 us

profile of v2, /device:TPU:5, one launch (start us, length us, event | category | flops | bytes accessed | tf_op | source)
XLA Modules:
  0.0 178.3 jit_solution(9523151179987106716)
XLA Ops:
  1.3 1.4 copy.16.jobc_ref
  2.7 168.6 %shard_map.147 = (bf16[128,1024]{1,0:T(8,128)(2,1)}, bf16[128,8192]{1,0:T(8,128)(2,1)}, f32[64,8192]{1,0:T(8,128)}, f32[64,1024]{1,0:T(8,128)}) custom-call(s32[1]{0:T(128)S(6)} %copy.21.rank_ref, s32[128,1]{1,0:T(8,128)} %copy.16.jobc_ref, s32[1,128]{1,0:T(1,128)} %bitcast.11, s32[320,1]{1,0:T(8,128)} %constant.10.clone.keyc_ref, ...), custom_call_target="tpu_custom_call" | custom-call | flops 16000000000 | bytes 16777216 | tf_op jit(solution)/shard_map/pallas_call | solution.py:444
  171.3 1.7 copy.22
  173.0 0.0 copy-start
  173.0 3.2 %copy.23 = bf16[128,8192]{1,0:T(8,128)(2,1)} copy(bf16[128,8192]{1,0:T(8,128)(2,1)} %get-tuple-element.17) | data formatting | bytes 4194304
  176.2 0.0 copy-done
  176.2 0.0 copy-start.1
  176.2 1.3 copy.24
  177.6 0.0 copy-done.1
  177.6 0.7 copy.25
Async XLA Ops:
  173.0 3.2 %copy-start = (f32[64,8192]{1,0:T(8,128)S(1)}, f32[64,8192]{1,0:T(8,128)}, u32[]{:S(2)}) copy-start(f32[64,8192]{1,0:T(8,128)} %get-tuple-element.10) | copy-start | bytes 6291460
  176.2 1.3 copy-start.1

commit v3 on v2

--- a/solution.py
+++ b/solution.py
@@ -9,7 +9,7 @@
 from jax.sharding import PartitionSpec as P
 
 CHUNKS = 8
-PIECES = 2
+PIECES = 4
 BF16 = jnp.bfloat16
 F32 = jnp.float32
 MESH = pl.DeviceIdType.MESH
@@ -23,7 +23,6 @@
     n,
     cap,
     rank_ref,
-    jobc_ref,
     jobr_ref,
     keyc_ref,
     keyr_ref,
@@ -91,8 +90,8 @@
     pair = lax.axis_size("groups") % 2 == 0
     group = lax.axis_index("groups")
     other = group + 1 - 2 * lax.rem(group, 2) if pair else group
-    mine = [lax.rem(group, 2)] if pair else list(range(PIECES))
-    theirs = [1 - lax.rem(group, 2)] if pair else []
+    mine = [lax.rem(group, 2) * 2 + v for v in range(2)] if pair else list(range(PIECES))
+    theirs = [2 - lax.rem(group, 2) * 2 + v for v in range(2)] if pair else []
 
     if pair:
         pl.semaphore_signal(
@@ -136,12 +135,11 @@
     for p in range(PIECES):
         w_copy(me, p, 3, core).start()
 
-    jc = jobc_ref[...]
     jr = jobr_ref[...]
-    same = jc == jr
     ri = lax.broadcasted_iota(jnp.int32, (tl, tl), 0)
     ci = lax.broadcasted_iota(jnp.int32, (tl, tl), 1)
-    one = jnp.where(same, 1.0, 0.0)
+    jc = jnp.sum(jnp.where(ri == ci, jr, 0).astype(F32), axis=1, keepdims=True).astype(jnp.int32)
+    one = jnp.where(jc == jr, 1.0, 0.0)
     pos_c = jnp.sum(jnp.where(ci < ri, one, 0.0), axis=1, keepdims=True).astype(jnp.int32)
     pos_r = jnp.sum(jnp.where(ri < ci, one, 0.0), axis=0, keepdims=True).astype(jnp.int32)
     slot_c = jc * cap + pos_c
@@ -437,8 +435,8 @@
     consts = [jnp.asarray(v, jnp.int32) for v in consts]
 
     vmem = pl.BlockSpec(memory_space=pltpu.VMEM)
-    args = (rank, job, job.reshape(1, tl), *consts, tokens, gradient, weight, down[0].T, up[0])
-    specs = [pl.BlockSpec(memory_space=pltpu.SMEM)] + [vmem] * 9
+    args = (rank, job.reshape(1, tl), *consts, tokens, gradient, weight, down[0].T, up[0])
+    specs = [pl.BlockSpec(memory_space=pltpu.SMEM)] + [vmem] * 8
     specs += [pl.BlockSpec(memory_space=pl.ANY)] + [vmem] * 2
     dma = pltpu.SemaphoreType.DMA
     values, grad_in, d_down, d_up = pl.pallas_call(

time: 180 us -> 177 us (0.983)
    unnamed x9 -> x8, local copies, waits for them, and re-layouts: 8.33 us -> 6.94 us
where the time goes in v3:
time: 177 us
  Pallas kernels  169 us (95%)
  local copies, waits for them, and re-layouts  6.94 us (4%)
    pallas_call x1, Pallas kernels, shards(): pl.pallas_call(functools.partial(kernel, n, cap), out_shape=(jax.ShapeDty...  169 us
    unnamed x8, local copies, waits for them, and re-layouts  6.94 us

profile of v3, /device:TPU:5, one launch (start us, length us, event | category | flops | bytes accessed | tf_op | source)
XLA Modules:
  0.0 176.8 jit_solution(17442526593970684417)
XLA Ops:
  1.3 168.6 %shard_map.147 = (bf16[128,1024]{1,0:T(8,128)(2,1)}, bf16[128,8192]{1,0:T(8,128)(2,1)}, f32[64,8192]{1,0:T(8,128)}, f32[64,1024]{1,0:T(8,128)}) custom-call(s32[1]{0:T(128)S(6)} %copy.20.rank_ref, s32[1,128]{1,0:T(1,128)} %bitcast.13, s32[320,1]{1,0:T(8,128)} %constant.10.clone.keyc_ref, s32[1,320]{1,0:T(1,128)} %constant.11.clone.keyr_ref, ...), custom_call_target="tpu_custom_call" | custom-call | flops 16000000000 | bytes 16777216 | tf_op jit(solution)/shard_map/pallas_call | solution.py:442
  169.8 1.7 copy.21
  171.5 0.0 copy-start
  171.5 3.2 %copy.22 = bf16[128,8192]{1,0:T(8,128)(2,1)} copy(bf16[128,8192]{1,0:T(8,128)(2,1)} %get-tuple-element.17) | data formatting | bytes 4194304
  174.8 0.0 copy-done
  174.8 0.0 copy-start.1
  174.8 1.3 copy.23
  176.1 0.0 copy-done.1
  176.1 0.7 copy.24
Async XLA Ops:
  171.5 3.2 %copy-start = (f32[64,8192]{1,0:T(8,128)S(1)}, f32[64,8192]{1,0:T(8,128)}, u32[]{:S(2)}) copy-start(f32[64,8192]{1,0:T(8,128)} %get-tuple-element.10) | copy-start | bytes 6291460
  174.8 1.3 copy-start.1
